TPU v7x, 256 devices: a whole 4x4x8 slice. The times are simulated.
256 devices in a mesh: row: 8 (over y, x_hi), col: 32 (over z, x_lo, core).
Axes of the slice: x: 4 (x_hi: 2, x_lo: 2; x = x_hi * 2 + x_lo), y: 4, z: 8, core: 2. Of those that a mesh axis runs over, the one named last changes fastest.
Arguments:
- cells: bfloat16 [2, 512, 512, 256], P(None, 'row', 'col'), may hold values from -6 to 6
- w_row_qkv: bfloat16 [256, 768], replicated, may hold values from -0.375 to 0.375
- w_row_out: bfloat16 [256, 256], replicated, may hold values from -0.375 to 0.375
- w_col_qkv: bfloat16 [256, 768], replicated, may hold values from -0.375 to 0.375
- w_col_out: bfloat16 [256, 256], replicated, may hold values from -0.375 to 0.375
- w_up: bfloat16 [256, 1024], replicated, may hold values from -0.375 to 0.375
- w_down: bfloat16 [1024, 256], replicated, may hold values from -0.1875 to 0.1875
Outputs:
- updated: bfloat16 [2, 512, 512, 256], P(None, 'row', 'col')
All inputs are finite; a program needn't handle non-finite values.
Results may differ from a plain program's by a relative error of at most 0.009.
Values may be sent and summed in bfloat16 or wider, within the bound.
A program may use at most 64 MiB of HBM per device.

v0:
```python
import jax
import jax.numpy as jnp
from jax import lax
from jax.sharding import PartitionSpec as P

HEADS = 8


eps = 1e-06


def rms(v32):
    return v32 * lax.rsqrt(jnp.mean(v32 * v32, axis=-1, keepdims=True) + eps)


def project(seq, w_qkv):
    width = seq.shape[-1]
    normed = rms(seq.astype(jnp.float32)).astype(jnp.bfloat16)
    mixed = jnp.dot(normed, w_qkv, preferred_element_type=jnp.float32)
    query = rms(mixed[..., :width]).astype(jnp.bfloat16)
    keys = rms(mixed[..., width : 2 * width]).astype(jnp.bfloat16)
    values = mixed[..., 2 * width :].astype(jnp.bfloat16)
    return (query, keys, values)


def one_sequence(triple):
    query, keys, values = triple
    length, width = query.shape
    size = width // HEADS
    q3 = query.reshape(length, HEADS, size)
    k3 = keys.reshape(length, HEADS, size)
    v3 = values.reshape(length, HEADS, size)
    scores = jnp.einsum("lgd,mgd->glm", q3, k3, preferred_element_type=jnp.float32) * size ** (-0.5)
    probs = jnp.exp(scores)
    total = jnp.sum(probs, axis=-1)
    summed = jnp.einsum(
        "glm,mgd->lgd", probs.astype(jnp.bfloat16), v3, preferred_element_type=jnp.float32
    )
    attended = summed / jnp.transpose(total)[:, :, None]
    return attended.reshape(length, width).astype(jnp.bfloat16)


def finish(seq, attended, w_out):
    out = jnp.dot(attended, w_out, preferred_element_type=jnp.float32)
    return (seq.astype(jnp.float32) + out).astype(jnp.bfloat16)


def attend(seq, w_qkv, w_out):
    query, keys, values = project(seq, w_qkv)
    attended = lax.map(one_sequence, (query, keys, values))
    return finish(seq, attended, w_out)


def body(cells, w_row_qkv, w_row_out, w_col_qkv, w_col_out, w_up, w_down):
    part = lax.all_to_all(cells, "col", split_axis=1, concat_axis=2, tiled=True)
    count, nrows, ncols, feats = part.shape
    done = attend(part.reshape(count * nrows, ncols, feats), w_row_qkv, w_row_out)
    rows_layout = done.reshape(count, nrows, ncols, feats)
    back_home = lax.all_to_all(rows_layout, "col", split_axis=2, concat_axis=1, tiled=True)
    part = lax.all_to_all(back_home, "row", split_axis=2, concat_axis=1, tiled=True)
    count, nrows, ncols, feats = part.shape
    turned = jnp.transpose(part, (0, 2, 1, 3)).reshape(count * ncols, nrows, feats)
    done = attend(turned, w_col_qkv, w_col_out).reshape(count, ncols, nrows, feats)
    cols_layout = jnp.transpose(done, (0, 2, 1, 3))
    tile = lax.all_to_all(cols_layout, "row", split_axis=1, concat_axis=2, tiled=True)
    normed = rms(tile.astype(jnp.float32)).astype(jnp.bfloat16)
    hidden = jax.nn.gelu(
        jnp.dot(normed, w_up, preferred_element_type=jnp.float32), approximate=True
    ).astype(jnp.bfloat16)
    down = jnp.dot(hidden, w_down, preferred_element_type=jnp.float32)
    return (tile.astype(jnp.float32) + down).astype(jnp.bfloat16)


def solution(mesh):
    return jax.shard_map(
        body,
        mesh=mesh,
        in_specs=(P(None, "row", "col", None), P(), P(), P(), P(), P(), P()),
        out_specs=P(None, "row", "col", None),
        check_vma=False,
    )
```

profile of v0, /device:TPU:1, one launch (start us, length us, event | category | flops | bytes accessed | tf_op | source)
XLA Modules:
  0.0 250.9 jit_solution(14275024946454694118)
XLA Ops:
  0.0 2.4 copy.129
  2.4 11.1 %all-to-all-start = ((bf16[2,64,16,256]{3,2,0,1:T(8,128)(2,1)}), bf16[2,64,16,256]{3,2,0,1:T(8,128)(2,1)S(1)}, u32[]{:S(2)}, u32[]{:S(2)}) async-start(bf16[2,64,16,256]{3,2,0,1:T(8,128)(2,1)} %copy.129), calls=%async_computation | async-start | bytes 2097152 | tf_op jit(solution)/shard_map/all_to_all | solution.py:55
  13.5 28.1 %all-to-all-done = bf16[2,64,16,256]{3,2,0,1:T(8,128)(2,1)S(1)} async-done(((bf16[2,64,16,256]{3,2,0,1:T(8,128)(2,1)}), bf16[2,64,16,256]{3,2,0,1:T(8,128)(2,1)S(1)}, u32[]{:S(2)}, u32[]{:S(2)}) %all-to-all-start) | async-done | bytes 1048608 | tf_op jit(solution)/shard_map/all_to_all | solution.py:55
  41.6 1.0 copy-done.1
  42.6 1.6 copy.130
  45.0 1.0 fusion.45
  46.6 1.2 slice.43
  47.8 1.7 multiply_convert_fusion.4
  49.5 1.1 broadcast.118.clone
  50.6 50.4 %while.20 = (s32[]{:T(128)}, bf16[4,512,256]{1,2,0:T(8,128)(2,1)}, bf16[4,512,256]{2,1,0:T(8,128)(2,1)}, bf16[4,512,256]{2,1,0:T(8,128)(2,1)}, bf16[4,512,256]{2,1,0:T(8,128)(2,1)}, /*index=5*/s32[]{:T(128)}) while((s32[]{:T(128)}, bf16[4,512,256]{1,2,0:T(8,128)(2,1)}, bf16[4,512,256]{2,1,0:T(8,128)(2,1)}, bf16[4,512,256]{2,1,0:T(8,128)(2,1)}, ...), condition=%wide.region_5.6_spmd, body=%wide.region_3.5_spmd.sunk | while | flops 277082112 | bytes 21529164 | solution.py:50
  50.6 1.1 constant_dynamic-slice_fusion.11
  52.0 4.6 %fusion.87 = (f32[8,512]{1,0:T(8,128)S(1)}, f32[8,512,512]{1,2,0:T(8,128)}) fusion(bf16[512,8,32]{0,2,1:T(8,128)(2,1)S(1)} %bitcast.134, bf16[512,8,32]{0,2,1:T(8,128)(2,1)S(1)} %bitcast.136), kind=kOutput, calls=%fused_computation.1.clone.1 | convolution fusion | flops 138407936 | bytes 8929280 | tf_op jit(solution)/shard_map/while/body/eval_jaxpr/lgd,mgd->glm/dot_general | solution.py:33
  56.6 1.0 constant_dynamic-slice_fusion.10
  57.7 4.7 %fusion.88 = bf16[512,8,32]{0,2,1:T(8,128)(2,1)S(1)} fusion(bf16[512,8,32]{0,2,1:T(8,128)(2,1)S(1)} %bitcast.138, f32[8,512,512]{1,2,0:T(8,128)} %get-tuple-element.236, f32[512,8]{0,1:T(8,128)S(1)} %bitcast.153), kind=kOutput, calls=%fused_computation.7.clone.1 | convolution fusion | flops 138674176 | bytes 8929280 | tf_op jit(solution)/shard_map/while/body/eval_jaxpr/glm,mgd->lgd/dot_general | solution.py:36
  62.5 0.7 constant_dynamic-update-slice_fusion.4
  63.2 1.1 constant_dynamic-slice_fusion.11
  64.6 4.6 %fusion.87 = (f32[8,512]{1,0:T(8,128)S(1)}, f32[8,512,512]{1,2,0:T(8,128)}) fusion(bf16[512,8,32]{0,2,1:T(8,128)(2,1)S(1)} %bitcast.134, bf16[512,8,32]{0,2,1:T(8,128)(2,1)S(1)} %bitcast.136), kind=kOutput, calls=%fused_computation.1.clone.1 | convolution fusion | flops 138407936 | bytes 8929280 | tf_op jit(solution)/shard_map/while/body/eval_jaxpr/lgd,mgd->glm/dot_general | solution.py:33
  69.2 1.0 constant_dynamic-slice_fusion.10
  70.3 4.7 %fusion.88 = bf16[512,8,32]{0,2,1:T(8,128)(2,1)S(1)} fusion(bf16[512,8,32]{0,2,1:T(8,128)(2,1)S(1)} %bitcast.138, f32[8,512,512]{1,2,0:T(8,128)} %get-tuple-element.236, f32[512,8]{0,1:T(8,128)S(1)} %bitcast.153), kind=kOutput, calls=%fused_computation.7.clone.1 | convolution fusion | flops 138674176 | bytes 8929280 | tf_op jit(solution)/shard_map/while/body/eval_jaxpr/glm,mgd->lgd/dot_general | solution.py:36
  75.1 0.7 constant_dynamic-update-slice_fusion.4
  75.8 1.1 constant_dynamic-slice_fusion.11
  77.2 4.6 %fusion.87 = (f32[8,512]{1,0:T(8,128)S(1)}, f32[8,512,512]{1,2,0:T(8,128)}) fusion(bf16[512,8,32]{0,2,1:T(8,128)(2,1)S(1)} %bitcast.134, bf16[512,8,32]{0,2,1:T(8,128)(2,1)S(1)} %bitcast.136), kind=kOutput, calls=%fused_computation.1.clone.1 | convolution fusion | flops 138407936 | bytes 8929280 | tf_op jit(solution)/shard_map/while/body/eval_jaxpr/lgd,mgd->glm/dot_general | solution.py:33
  81.8 1.0 constant_dynamic-slice_fusion.10
  82.9 4.7 %fusion.88 = bf16[512,8,32]{0,2,1:T(8,128)(2,1)S(1)} fusion(bf16[512,8,32]{0,2,1:T(8,128)(2,1)S(1)} %bitcast.138, f32[8,512,512]{1,2,0:T(8,128)} %get-tuple-element.236, f32[512,8]{0,1:T(8,128)S(1)} %bitcast.153), kind=kOutput, calls=%fused_computation.7.clone.1 | convolution fusion | flops 138674176 | bytes 8929280 | tf_op jit(solution)/shard_map/while/body/eval_jaxpr/glm,mgd->lgd/dot_general | solution.py:36
  88.4 1.1 constant_dynamic-slice_fusion.11
  89.8 4.6 %fusion.87 = (f32[8,512]{1,0:T(8,128)S(1)}, f32[8,512,512]{1,2,0:T(8,128)}) fusion(bf16[512,8,32]{0,2,1:T(8,128)(2,1)S(1)} %bitcast.134, bf16[512,8,32]{0,2,1:T(8,128)(2,1)S(1)} %bitcast.136), kind=kOutput, calls=%fused_computation.1.clone.1 | convolution fusion | flops 138407936 | bytes 8929280 | tf_op jit(solution)/shard_map/while/body/eval_jaxpr/lgd,mgd->glm/dot_general | solution.py:33
  94.4 1.0 constant_dynamic-slice_fusion.10
  95.5 4.7 %fusion.88 = bf16[512,8,32]{0,2,1:T(8,128)(2,1)S(1)} fusion(bf16[512,8,32]{0,2,1:T(8,128)(2,1)S(1)} %bitcast.138, f32[8,512,512]{1,2,0:T(8,128)} %get-tuple-element.236, f32[512,8]{0,1:T(8,128)S(1)} %bitcast.153), kind=kOutput, calls=%fused_computation.7.clone.1 | convolution fusion | flops 138674176 | bytes 8929280 | tf_op jit(solution)/shard_map/while/body/eval_jaxpr/glm,mgd->lgd/dot_general | solution.py:36
  101.0 1.7 add_convert_fusion.2
  102.7 1.1 copy.138
  103.8 32.2 %all_to_all.48 = bf16[2,2,512,256]{3,1,0,2:T(2,128)(2,1)S(1)} all-to-all(bf16[2,2,512,256]{3,1,0,2:T(2,128)(2,1)S(1)} %copy.138), channel_id=1, replica_groups=mesh['row'=8,'col'=32] {'col'}, dimensions={2} | all-to-all | bytes 2097152 | tf_op jit(solution)/shard_map/all_to_all | solution.py:59
  136.6 21.9 %all_to_all.49 = bf16[2,64,16,256]{3,1,0,2:T(8,128)(2,1)S(1)} all-to-all(bf16[2,64,16,256]{3,1,0,2:T(8,128)(2,1)S(1)} %copy.141), channel_id=1, replica_groups=mesh['row'=8,'col'=32] {'row'}, dimensions={2} | all-to-all | bytes 2097152 | tf_op jit(solution)/shard_map/all_to_all | solution.py:60
  160.3 1.0 fusion.46
  161.9 1.2 slice.42
  163.1 1.7 multiply_convert_fusion.1
  164.8 1.1 broadcast.118
  165.9 50.4 %while.21 = (s32[]{:T(128)}, bf16[4,512,256]{1,2,0:T(8,128)(2,1)}, bf16[4,512,256]{2,1,0:T(8,128)(2,1)}, bf16[4,512,256]{2,1,0:T(8,128)(2,1)}, bf16[4,512,256]{2,1,0:T(8,128)(2,1)}, /*index=5*/s32[]{:T(128)}) while((s32[]{:T(128)}, bf16[4,512,256]{1,2,0:T(8,128)(2,1)}, bf16[4,512,256]{2,1,0:T(8,128)(2,1)}, bf16[4,512,256]{2,1,0:T(8,128)(2,1)}, ...), condition=%wide.region_11.12_spmd, body=%wide.region_9.11_spmd.sunk | while | flops 277082112 | bytes 21529164 | solution.py:50
  165.9 1.1 constant_dynamic-slice_fusion.13
  167.3 4.6 %fusion.93 = (f32[8,512]{1,0:T(8,128)S(1)}, f32[8,512,512]{1,2,0:T(8,128)}) fusion(bf16[512,8,32]{0,2,1:T(8,128)(2,1)S(1)} %bitcast.135, bf16[512,8,32]{0,2,1:T(8,128)(2,1)S(1)} %bitcast.137), kind=kOutput, calls=%fused_computation.14.clone.1 | convolution fusion | flops 138407936 | bytes 8929280 | tf_op jit(solution)/shard_map/while/body/eval_jaxpr/lgd,mgd->glm/dot_general | solution.py:33
  171.9 1.0 constant_dynamic-slice_fusion.12
  173.1 4.7 %fusion.94 = bf16[512,8,32]{0,2,1:T(8,128)(2,1)S(1)} fusion(bf16[512,8,32]{0,2,1:T(8,128)(2,1)S(1)} %bitcast.139, f32[8,512,512]{1,2,0:T(8,128)} %get-tuple-element.245, f32[512,8]{0,1:T(8,128)S(1)} %bitcast.154), kind=kOutput, calls=%fused_computation.20.clone.1 | convolution fusion | flops 138674176 | bytes 8929280 | tf_op jit(solution)/shard_map/while/body/eval_jaxpr/glm,mgd->lgd/dot_general | solution.py:36
  177.8 0.7 constant_dynamic-update-slice_fusion.5
  178.5 1.1 constant_dynamic-slice_fusion.13
  179.9 4.6 %fusion.93 = (f32[8,512]{1,0:T(8,128)S(1)}, f32[8,512,512]{1,2,0:T(8,128)}) fusion(bf16[512,8,32]{0,2,1:T(8,128)(2,1)S(1)} %bitcast.135, bf16[512,8,32]{0,2,1:T(8,128)(2,1)S(1)} %bitcast.137), kind=kOutput, calls=%fused_computation.14.clone.1 | convolution fusion | flops 138407936 | bytes 8929280 | tf_op jit(solution)/shard_map/while/body/eval_jaxpr/lgd,mgd->glm/dot_general | solution.py:33
  184.5 1.0 constant_dynamic-slice_fusion.12
  185.7 4.7 %fusion.94 = bf16[512,8,32]{0,2,1:T(8,128)(2,1)S(1)} fusion(bf16[512,8,32]{0,2,1:T(8,128)(2,1)S(1)} %bitcast.139, f32[8,512,512]{1,2,0:T(8,128)} %get-tuple-element.245, f32[512,8]{0,1:T(8,128)S(1)} %bitcast.154), kind=kOutput, calls=%fused_computation.20.clone.1 | convolution fusion | flops 138674176 | bytes 8929280 | tf_op jit(solution)/shard_map/while/body/eval_jaxpr/glm,mgd->lgd/dot_general | solution.py:36
  190.4 0.7 constant_dynamic-update-slice_fusion.5
  191.1 1.1 constant_dynamic-slice_fusion.13
  192.5 4.6 %fusion.93 = (f32[8,512]{1,0:T(8,128)S(1)}, f32[8,512,512]{1,2,0:T(8,128)}) fusion(bf16[512,8,32]{0,2,1:T(8,128)(2,1)S(1)} %bitcast.135, bf16[512,8,32]{0,2,1:T(8,128)(2,1)S(1)} %bitcast.137), kind=kOutput, calls=%fused_computation.14.clone.1 | convolution fusion | flops 138407936 | bytes 8929280 | tf_op jit(solution)/shard_map/while/body/eval_jaxpr/lgd,mgd->glm/dot_general | solution.py:33
  197.1 1.0 constant_dynamic-slice_fusion.12
  198.2 4.7 %fusion.94 = bf16[512,8,32]{0,2,1:T(8,128)(2,1)S(1)} fusion(bf16[512,8,32]{0,2,1:T(8,128)(2,1)S(1)} %bitcast.139, f32[8,512,512]{1,2,0:T(8,128)} %get-tuple-element.245, f32[512,8]{0,1:T(8,128)S(1)} %bitcast.154), kind=kOutput, calls=%fused_computation.20.clone.1 | convolution fusion | flops 138674176 | bytes 8929280 | tf_op jit(solution)/shard_map/while/body/eval_jaxpr/glm,mgd->lgd/dot_general | solution.py:36
  203.0 0.7 constant_dynamic-update-slice_fusion.5
  203.7 1.1 constant_dynamic-slice_fusion.13
  205.1 4.6 %fusion.93 = (f32[8,512]{1,0:T(8,128)S(1)}, f32[8,512,512]{1,2,0:T(8,128)}) fusion(bf16[512,8,32]{0,2,1:T(8,128)(2,1)S(1)} %bitcast.135, bf16[512,8,32]{0,2,1:T(8,128)(2,1)S(1)} %bitcast.137), kind=kOutput, calls=%fused_computation.14.clone.1 | convolution fusion | flops 138407936 | bytes 8929280 | tf_op jit(solution)/shard_map/while/body/eval_jaxpr/lgd,mgd->glm/dot_general | solution.py:33
  209.7 1.0 constant_dynamic-slice_fusion.12
  210.8 4.7 %fusion.94 = bf16[512,8,32]{0,2,1:T(8,128)(2,1)S(1)} fusion(bf16[512,8,32]{0,2,1:T(8,128)(2,1)S(1)} %bitcast.139, f32[8,512,512]{1,2,0:T(8,128)} %get-tuple-element.245, f32[512,8]{0,1:T(8,128)S(1)} %bitcast.154), kind=kOutput, calls=%fused_computation.20.clone.1 | convolution fusion | flops 138674176 | bytes 8929280 | tf_op jit(solution)/shard_map/while/body/eval_jaxpr/glm,mgd->lgd/dot_general | solution.py:36
  215.6 0.7 constant_dynamic-update-slice_fusion.5
  216.3 1.7 add_convert_fusion.1
  218.0 1.1 copy.168
  219.1 17.1 %all_to_all.50 = bf16[2,512,2,256]{3,2,0,1:T(2,128)(2,1)S(1)} all-to-all(bf16[2,512,2,256]{3,2,0,1:T(2,128)(2,1)S(1)} %bitcast.150), channel_id=1, replica_groups=mesh['row'=8,'col'=32] {'row'}, dimensions={1} | all-to-all | bytes 2097152 | tf_op jit(solution)/shard_map/all_to_all | solution.py:65
  236.3 2.5 %copy_bitcast_fusion = f32[2,64,8,2,256]{4,3,2,1,0:T(2,128)} fusion(bf16[2,8,64,2,256]{4,3,0,2,1:T(2,128)(2,1)S(1)} %bitcast.145), kind=kLoop, calls=%fused_computation.42 | loop fusion | flops 524288 | bytes 3145728 | tf_op jit(solution)/shard_map/convert_element_type | solution.py:71
  238.8 3.7 %reshape.171 = f32[2,64,16,256]{3,2,1,0:T(8,128)} reshape(f32[2,64,8,2,256]{4,3,2,1,0:T(2,128)} %copy_bitcast_fusion) | data formatting | bytes 4194304 | tf_op jit(solution)/shard_map/convert_element_type | solution.py:71
  242.5 1.7 multiply_reduce_fusion
  244.6 6.3 %add_convert_fusion = bf16[2,64,16,256]{3,2,1,0:T(8,128)(2,1)} fusion(f32[2,64,16,256]{3,2,1,0:T(8,128)} %reshape.171, f32[2,64,16]{2,1,0:T(8,128)S(1)} %copy.153, bf16[1024,256]{1,0:T(8,128)(2,1)S(1)} %copy-done, bf16[256,1024]{1,0:T(8,128)(2,1)S(1)} %copy-done.7), kind=kOutput, calls=%fused_computation.43 | convolution fusion | flops 2168455168 | bytes 4202496 | tf_op jit(solution)/shard_map/dot_general | solution.py:70
  (68 shorter events, 9.5 us)
Async XLA Ops:
  0.0 244.6 %copy-start = (bf16[1024,256]{1,0:T(8,128)(2,1)S(1)}, bf16[1024,256]{1,0:T(8,128)(2,1)}, u32[]{:S(2)}) copy-start(bf16[1024,256]{1,0:T(8,128)(2,1)} %param.17) | copy-start | bytes 1572868
  2.4 39.2 %all-to-all-start = ((bf16[2,64,16,256]{3,2,0,1:T(8,128)(2,1)}), bf16[2,64,16,256]{3,2,0,1:T(8,128)(2,1)S(1)}, u32[]{:S(2)}, u32[]{:S(2)}) async-start(bf16[2,64,16,256]{3,2,0,1:T(8,128)(2,1)} %copy.129), calls=%async_computation | async-start | bytes 2097152 | tf_op jit(solution)/shard_map/all_to_all | solution.py:55
  41.6 1.0 copy-start.1
  42.6 1.6 copy-start.2
  42.6 2.4 copy-start.3
  50.6 50.4 %copy-start.5 = (bf16[256,256]{1,0:T(8,128)(2,1)S(1)}, bf16[256,256]{1,0:T(8,128)(2,1)}, u32[]{:S(2)}) copy-start(bf16[256,256]{1,0:T(8,128)(2,1)} %param.13) | copy-start | bytes 393220
  159.3 1.0 copy-start.4
  165.9 50.4 %copy-start.6 = (bf16[256,256]{1,0:T(8,128)(2,1)S(1)}, bf16[256,256]{1,0:T(8,128)(2,1)}, u32[]{:S(2)}) copy-start(bf16[256,256]{1,0:T(8,128)(2,1)} %param.15) | copy-start | bytes 393220
  242.5 2.1 copy-start.7
where the time goes:
time: 254 us; the launch traced here: 251 us
  matrix products  86.9 us (34%)
  blocking collectives  71.2 us (28%)
  local copies, waits for them, and re-layouts  43.1 us (17%)
  waiting for transfers between devices  28.1 us (11%)
  starting transfers between devices  11.1 us (4%)
  other arithmetic  10 us (4%)
    dot_general x8, matrix products, one_sequence(): jnp.einsum('glm,mgd->lgd', probs.astype(jnp.bfloat16), v3, preferred_elem...  38 us
    dot_general x8, matrix products, one_sequence(): jnp.einsum('lgd,mgd->glm', q3, k3, preferred_element_type=jnp.float32)  37.2 us
    all_to_all x1, blocking collectives, body(): lax.all_to_all(rows_layout, 'col', split_axis=2, concat_axis=1, tiled=True)  32.2 us
    all_to_all x1, waiting for transfers between devices, body(): part = lax.all_to_all(cells, 'col', split_axis=1, concat_axis=2, tiled=True)  28.1 us
    all_to_all x1, blocking collectives, body(): lax.all_to_all(back_home, 'row', split_axis=2, concat_axis=1, tiled=True)  21.9 us
    dynamic_slice x40, local copies, waits for them, and re-layouts, attend(): attended = lax.map(one_sequence, (query, keys, values))  19.7 us
    all_to_all x1, blocking collectives, body(): lax.all_to_all(cols_layout, 'row', split_axis=1, concat_axis=2, tiled=True)  17.1 us
    all_to_all x1, starting transfers between devices, body(): part = lax.all_to_all(cells, 'col', split_axis=1, concat_axis=2, tiled=True)  11.1 us
  transfers between devices with their start and end apart: 1, of which 1 were waited for; matrix products, arithmetic and copies ran while one was open for 0% of the time, Pallas kernels for 0%

commit v1 on v0

v1 whole, which is shorter than its diff:
```python
import functools
import math

import jax
import jax.numpy as jnp
from jax import lax
from jax.experimental import pallas as pl
from jax.experimental.pallas import tpu as pltpu
from jax.sharding import PartitionSpec as P

MESH = pl.DeviceIdType.MESH
BF = jnp.bfloat16
F32 = jnp.float32
HEADS = 8
EPS = 1e-06


def rms(v, scale=None):
    r = lax.rsqrt(jnp.mean(v * v, axis=-1, keepdims=True) + EPS)
    return v * (r if scale is None else r * scale)


def mm(a, b):
    return jnp.dot(a, b, preferred_element_type=F32)


def mm_nt(a, b):
    return lax.dot_general(a, b, (((1,), (1,)), ((), ())), preferred_element_type=F32)


def permutation(size, low, ref):
    o = lax.broadcasted_iota(jnp.int32, (size, size), 0)
    s = lax.broadcasted_iota(jnp.int32, (size, size), 1)
    high = size // low
    hit = s == (o & (high - 1)) * low + lax.shift_right_logical(o, int(math.log2(high)))
    ref[...] = jnp.where(hit, 1.0, 0.0).astype(BF)


def kernel(
    nr, nc,
    x_hbm, wrq, wro, wcq, wco, wup, wdn,
    out_ref,
    wqkv, wo, up, down, seqs, stash, rowout, home2, home2t, colout, home3, res,
    q_s, k_s, w_s, perm_in, perm_out,
    w_sem, in_send, in_recv, z_send, z_recv, c_send, c_recv, b_send, b_recv,
):
    r = lax.axis_index("row")
    c = lax.axis_index("col")
    length, width = seqs.shape[1], seqs.shape[2]
    half = width // 2
    size = width // HEADS
    qscale = math.log2(math.e) / math.sqrt(size)

    weight_copies = [
        pltpu.make_async_copy(wrq, wqkv.at[0], w_sem.at[0]),
        pltpu.make_async_copy(wcq, wqkv.at[1], w_sem.at[1]),
        pltpu.make_async_copy(wro, wo.at[0], w_sem.at[2]),
        pltpu.make_async_copy(wco, wo.at[1], w_sem.at[3]),
        pltpu.make_async_copy(wup, up, w_sem.at[4]),
        pltpu.make_async_copy(wdn, down, w_sem.at[5]),
    ]
    for copy in weight_copies:
        copy.start()

    barrier = pltpu.get_barrier_semaphore()

    def greet_col(k, _):
        pl.semaphore_signal(
            barrier, inc=1, device_id={"col": lax.rem(c + k, nc)}, device_id_type=MESH
        )
        return 0

    def greet_row(k, _):
        pl.semaphore_signal(
            barrier, inc=1, device_id={"row": lax.rem(r + k, nr)}, device_id_type=MESH
        )
        return 0

    lax.fori_loop(1, nc, greet_col, 0)
    lax.fori_loop(1, nr, greet_row, 0)
    permutation(256, 8, perm_in)
    permutation(256, 16, perm_out)
    pl.semaphore_wait(barrier, nc + nr - 2)

    def tile(base, n):
        return pl.ds(pl.multiple_of(base, n), n)

    def send_in(s, _):
        m, i = lax.shift_right_logical(s, 1), s & 1

        def one(k, _):
            peer = lax.rem(c + k, nc)
            pltpu.make_async_remote_copy(
                src_ref=x_hbm.at[m, 2 * peer + i],
                dst_ref=seqs.at[s, tile(c * 16, 16)],
                send_sem=in_send.at[s],
                recv_sem=in_recv.at[s],
                device_id={"col": peer},
                device_id_type=MESH,
            ).start()
            return 0

        pltpu.make_async_copy(
            x_hbm.at[m, 2 * c + i], seqs.at[s, tile(c * 16, 16)], in_recv.at[s]
        ).start()
        lax.fori_loop(1, nc, one, 0)
        return 0

    lax.fori_loop(0, 4, send_in, 0)

    def send_back(q):
        def one(k, _):
            peer = lax.rem(c + k, nc)
            pltpu.make_async_remote_copy(
                src_ref=rowout.at[q, peer],
                dst_ref=home2.at[q, tile(c * 16, 16)],
                send_sem=z_send.at[q],
                recv_sem=z_recv.at[q],
                device_id={"col": peer},
                device_id_type=MESH,
            ).start()
            return 0

        pltpu.make_async_copy(rowout.at[q, c], home2.at[q, tile(c * 16, 16)], z_recv.at[q]).start()
        lax.fori_loop(1, nc, one, 0)

    def turn(q):
        pltpu.make_async_copy(home2.at[q], home2.at[q], z_recv.at[q]).wait()
        for b in range(2):
            moved = mm(perm_in[...], home2[q, b * 256 : (b + 1) * 256, :])
            home2t[q, :, b * 32 : (b + 1) * 32, :] = moved.reshape(8, 32, width).astype(BF)

        def one(k, _):
            peer = lax.rem(r + k, nr)
            pltpu.make_async_remote_copy(
                src_ref=home2t.at[q, peer],
                dst_ref=seqs.at[4 + q, tile(r * 64, 64)],
                send_sem=c_send.at[q],
                recv_sem=c_recv.at[q],
                device_id={"row": peer},
                device_id_type=MESH,
            ).start()
            return 0

        pltpu.make_async_copy(
            home2t.at[q, r], seqs.at[4 + q, tile(r * 64, 64)], c_recv.at[q]
        ).start()
        lax.fori_loop(1, nr, one, 0)

    def send_home(q):
        def one(k, _):
            peer = lax.rem(r + k, nr)
            pltpu.make_async_remote_copy(
                src_ref=colout.at[q, tile(peer * 64, 64)],
                dst_ref=home3.at[q, tile(r * 64, 64)],
                send_sem=b_send.at[q],
                recv_sem=b_recv.at[q],
                device_id={"row": peer},
                device_id_type=MESH,
            ).start()
            return 0

        pltpu.make_async_copy(
            colout.at[q, tile(r * 64, 64)], home3.at[q, tile(r * 64, 64)], b_recv.at[q]
        ).start()
        lax.fori_loop(1, nr, one, 0)

    lane_head = lax.shift_right_logical(
        lax.broadcasted_iota(jnp.int32, (1, width), 1), int(math.log2(size))
    )
    zero, one_ = jnp.zeros((), BF), jnp.ones((), BF)

    def attention(t):
        which = lax.shift_right_logical(t, 2)
        for b in range(0, length, 256):
            normed = rms(seqs[t, b : b + 256, :].astype(F32)).astype(BF)
            mixed = mm(normed, wqkv[which])
            q_s[b : b + 256, :] = rms(mixed[:, :width], qscale).astype(BF)
            k_s[b : b + 256, :] = rms(mixed[:, width : 2 * width]).astype(BF)
            values = mixed[:, 2 * width :].astype(BF)
            for h in range(HEADS):
                ones = jnp.where(lane_head == (h + 4) % 8, one_, zero)
                w_s[h * length + b : h * length + b + 256, :] = jnp.where(
                    lane_head == h, values, ones
                )
        queries, keys = q_s[...], k_s[...]
        sums = []
        for g in range(2):
            weights = []
            for h in range(4 * g, 4 * g + 4):
                scores = mm_nt(jnp.where(lane_head == h, queries, zero), keys)
                weights.append(jnp.exp2(scores).astype(BF))
            sums.append(
                mm(
                    jnp.concatenate(weights, axis=1),
                    w_s[4 * g * length : 4 * (g + 1) * length, :],
                )
            )
        attended = jnp.concatenate(
            [
                sums[0][:, :half] / sums[0][:, half:],
                sums[1][:, half:] / sums[1][:, :half],
            ],
            axis=1,
        ).astype(BF)
        return seqs[t].astype(F32) + mm(attended, wo[which])

    def feed_forward(q):
        pltpu.make_async_copy(home3.at[q], home3.at[q], b_recv.at[q]).wait()
        for b in range(0, length, 256):
            y = home3[q, b : b + 256, :].astype(F32)
            hidden = jax.nn.gelu(mm(rms(y).astype(BF), up[...]), approximate=True)
            res[q, b : b + 256, :] = (y + mm(hidden.astype(BF), down[...])).astype(BF)

    def finish(m):
        for b in range(4):
            parts = [
                res[2 * m + j, n * 64 + b * 16 : n * 64 + b * 16 + 16, :]
                for j in range(2)
                for n in range(8)
            ]
            moved = mm(perm_out[...], jnp.concatenate(parts, axis=0))
            out_ref[m, b * 16 : (b + 1) * 16] = moved.reshape(16, 16, width).astype(BF)

    weight_copies_done = [False]
    for copy in weight_copies:
        copy.wait()

    def step(t, _):
        @pl.when(t < 4)
        def _():
            pltpu.make_async_copy(seqs.at[t], seqs.at[t], in_recv.at[t & 3]).wait()

        @pl.when(t >= 4)
        def _():
            pltpu.make_async_copy(seqs.at[t], seqs.at[t], c_recv.at[t & 3]).wait()

        done = attention(t)

        @pl.when((t < 4) & ((t & 1) == 0))
        def _():
            stash[...] = done

        @pl.when((t < 4) & ((t & 1) == 1))
        def _():
            q = t - 1
            first = stash[...].reshape(32, 2, 8, width)
            second = done.reshape(32, 2, 8, width)
            for j in range(2):
                both = jnp.concatenate([first[:, j], second[:, j]], axis=1)
                rowout[q + j] = both.astype(BF)
            send_back(q)
            send_back(q + 1)

        @pl.when(t == 3)
        def _():
            turn(0)
            turn(1)

        @pl.when(t >= 4)
        def _():
            colout[t - 4] = done.astype(BF)
            send_home(t - 4)

        @pl.when(t == 5)
        def _():
            feed_forward(0)
            feed_forward(1)
            finish(0)
            turn(2)
            turn(3)

        return 0

    lax.fori_loop(0, 8, step, 0)
    feed_forward(2)
    feed_forward(3)
    finish(1)

    def drain(q, _):
        for ref, sem, rows in (
            (seqs, in_send, (nc - 1) * 16),
            (home2, z_send, (nc - 1) * 16),
            (colout, c_send, (nr - 1) * 64),
            (home3, b_send, (nr - 1) * 64),
        ):
            view = ref.at[q, pl.ds(0, rows)]
            pltpu.make_async_copy(view, view, sem.at[q]).wait()
        return 0

    lax.fori_loop(0, 4, drain, 0)


def solution(mesh):
    nr, nc = mesh.shape["row"], mesh.shape["col"]

    def body(cells, *weights):
        width = cells.shape[-1]
        ff = weights[4].shape[1]
        dma4 = pltpu.SemaphoreType.DMA((4,))
        return pl.pallas_call(
            functools.partial(kernel, nr, nc),
            out_shape=jax.ShapeDtypeStruct(cells.shape, BF),
            in_specs=[pl.BlockSpec(memory_space=pl.ANY)] * 7,
            out_specs=pl.BlockSpec(memory_space=pltpu.VMEM),
            scratch_shapes=[
                pltpu.VMEM((2, width, 3 * width), BF),
                pltpu.VMEM((2, width, width), BF),
                pltpu.VMEM((width, ff), BF),
                pltpu.VMEM((ff, width), BF),
                pltpu.VMEM((8, 512, width), BF),
                pltpu.VMEM((512, width), F32),
                pltpu.VMEM((4, 32, 16, width), BF),
                pltpu.VMEM((4, 512, width), BF),
                pltpu.VMEM((4, 8, 64, width), BF),
                pltpu.VMEM((4, 512, width), BF),
                pltpu.VMEM((4, 512, width), BF),
                pltpu.VMEM((4, 512, width), BF),
                pltpu.VMEM((512, width), BF),
                pltpu.VMEM((512, width), BF),
                pltpu.VMEM((HEADS * 512, width), BF),
                pltpu.VMEM((256, 256), BF),
                pltpu.VMEM((256, 256), BF),
                pltpu.SemaphoreType.DMA((6,)),
            ]
            + [dma4] * 8,
            compiler_params=pltpu.CompilerParams(
                collective_id=0, has_side_effects=True, vmem_limit_bytes=56 << 20
            ),
            name="axial",
        )(cells, *weights)

    return jax.shard_map(
        body,
        mesh=mesh,
        in_specs=(P(None, "row", "col", None),) + (P(),) * 6,
        out_specs=P(None, "row", "col", None),
        check_vma=False,
    )
```

time: 254 us -> 90.4 us (0.36)
  Pallas kernels: 0 us -> 87.4 us
  matrix products: 86.9 us -> 0 us
  blocking collectives: 71.2 us -> 0 us
  local copies, waits for them, and re-layouts: 43.1 us -> 2.26 us
  waiting for transfers between devices: 28.1 us -> 0 us
  starting transfers between devices: 11.1 us -> 0 us
  other arithmetic: 10 us -> 0 us
    pallas_call x0 -> x1, Pallas kernels: none -> 87.4 us  [body(): pl.pallas_call(functools.partial(kernel, nr, nc), out_shape=jax.ShapeDtyp...]
    dot_general x21 -> x0, matrix products: 86.9 us -> none  [the longest x8 38 us: one_sequence(): jnp.einsum('glm,mgd->lgd', probs.astype(jnp.bfloat16), v3, preferred_elem...]
    all_to_all x3 -> x0, blocking collectives: 71.2 us -> none  [the longest x1 32.2 us: body(): lax.all_to_all(rows_layout, 'col', split_axis=2, concat_axis=1, tiled=True)]
    all_to_all x1 -> x0, waiting for transfers between devices: 28.1 us -> none  [body(): part = lax.all_to_all(cells, 'col', split_axis=1, concat_axis=2, tiled=True)]
    dynamic_slice x40 -> x0, local copies, waits for them, and re-layouts: 19.7 us -> none  [attend(): attended = lax.map(one_sequence, (query, keys, values))]
    all_to_all x1 -> x0, starting transfers between devices: 11.1 us -> none  [body(): part = lax.all_to_all(cells, 'col', split_axis=1, concat_axis=2, tiled=True)]
    convert_element_type x4 -> x0, other arithmetic: 6.19 us -> none  [the longest x2 3.39 us: project(): keys = rms(mixed[..., width:2 * width]).astype(jnp.bfloat16)]
    dynamic_update_slice x8 -> x0, local copies, waits for them, and re-layouts: 5.81 us -> none  [attend(): attended = lax.map(one_sequence, (query, keys, values))]
  transfers between devices with their start and end apart: 1 -> 0, of which waited for: 1 -> 0; matrix products, arithmetic and copies ran while one was open for 0% -> 0% of each run, Pallas kernels for 0% -> 0%
where the time goes in v1:
time: 90.4 us; the launch traced here: 89.7 us
  Pallas kernels  87.4 us (97%)
  local copies, waits for them, and re-layouts  2.26 us (2%)
    pallas_call x1, Pallas kernels, body(): pl.pallas_call(functools.partial(kernel, nr, nc), out_shape=jax.ShapeDtyp...  87.4 us
    unnamed x1, local copies, waits for them, and re-layouts  2.26 us

profile of v1, /device:TPU:1, one launch (start us, length us, event | category | flops | bytes accessed | tf_op | source)
XLA Modules:
  0.0 89.7 jit_solution(214843237035965117)
XLA Ops:
  0.0 87.4 %axial.1 = bf16[2,64,16,256]{3,2,1,0:T(8,128)(2,1)} custom-call(bf16[2,64,16,256]{3,2,1,0:T(8,128)(2,1)} %x_hbm.1, bf16[256,768]{1,0:T(8,128)(2,1)} %wrq.1, bf16[256,256]{1,0:T(8,128)(2,1)} %wro.1, bf16[256,768]{1,0:T(8,128)(2,1)} %wcq.1, bf16[256,256]{1,0:T(8,128)(2,1)} %wco.1, bf16[256,1024]{1,0:T(8,128)(2,1)} %wup.1, bf16[1024,256]{1,0:T(8,128)(2,1)} %wdn.1), custom_call_target="tpu_custom_call" | custom-call | tf_op jit(solution)/shard_map/axial/pallas_call | solution.py:301
  87.4 2.3 %copy.9 = bf16[2,64,16,256]{3,2,1,0:T(8,128)(2,1)} copy(bf16[2,64,16,256]{3,2,1,0:T(8,128)(2,1)} %axial.1) | data formatting | bytes 2097152

commit v2 on v1

--- a/solution.py
+++ b/solution.py
@@ -28,16 +28,18 @@
     return lax.dot_general(a, b, (((1,), (1,)), ((), ())), preferred_element_type=F32)
 
 
-def permutation(size, low, ref):
-    o = lax.broadcasted_iota(jnp.int32, (size, size), 0)
-    s = lax.broadcasted_iota(jnp.int32, (size, size), 1)
-    high = size // low
-    hit = s == (o & (high - 1)) * low + lax.shift_right_logical(o, int(math.log2(high)))
-    ref[...] = jnp.where(hit, 1.0, 0.0).astype(BF)
+def permutation(ref, source):
+    o = lax.broadcasted_iota(jnp.int32, ref.shape, 0)
+    s = lax.broadcasted_iota(jnp.int32, ref.shape, 1)
+    ref[...] = jnp.where(s == source(o), 1.0, 0.0).astype(BF)
+
+
+def shr(v, n):
+    return lax.shift_right_logical(v, n)
 
 
 def kernel(
-    nr, nc,
+    nr, nc, nz,
     x_hbm, wrq, wro, wcq, wco, wup, wdn,
     out_ref,
     wqkv, wo, up, down, seqs, stash, rowout, home2, home2t, colout, home3, res,
@@ -46,6 +48,12 @@
 ):
     r = lax.axis_index("row")
     c = lax.axis_index("col")
+    z, corner = shr(c, 2), c & 3
+    place = r * 4 + corner
+
+    def in_plane(other):
+        return {"row": shr(other, 2), "col": z * 4 + (other & 3)}
+
     length, width = seqs.shape[1], seqs.shape[2]
     half = width // 2
     size = width // HEADS
@@ -70,23 +78,24 @@
         )
         return 0
 
-    def greet_row(k, _):
+    def greet_plane(k, _):
+        other = lax.rem(place + k, 4 * nr)
         pl.semaphore_signal(
-            barrier, inc=1, device_id={"row": lax.rem(r + k, nr)}, device_id_type=MESH
+            barrier, inc=1, device_id=in_plane(other), device_id_type=MESH
         )
         return 0
 
     lax.fori_loop(1, nc, greet_col, 0)
-    lax.fori_loop(1, nr, greet_row, 0)
-    permutation(256, 8, perm_in)
-    permutation(256, 16, perm_out)
-    pl.semaphore_wait(barrier, nc + nr - 2)
+    lax.fori_loop(1, 4 * nr, greet_plane, 0)
+    permutation(perm_in, lambda o: (shr(o, 4) & 1) * 128 + (o & 15) * 8 + shr(o, 5))
+    permutation(perm_out, lambda o: (o & 15) * 16 + shr(o, 4))
+    pl.semaphore_wait(barrier, nc - 1 + 4 * nr - 1)
 
     def tile(base, n):
         return pl.ds(pl.multiple_of(base, n), n)
 
     def send_in(s, _):
-        m, i = lax.shift_right_logical(s, 1), s & 1
+        m, i = shr(s, 1), s & 1
 
         def one(k, _):
             peer = lax.rem(c + k, nc)
@@ -110,42 +119,45 @@
 
     def send_back(q):
         def one(k, _):
-            peer = lax.rem(c + k, nc)
+            there = lax.rem(z + k, nz)
             pltpu.make_async_remote_copy(
-                src_ref=rowout.at[q, peer],
-                dst_ref=home2.at[q, tile(c * 16, 16)],
+                src_ref=rowout.at[q, there],
+                dst_ref=home2.at[q, z],
                 send_sem=z_send.at[q],
                 recv_sem=z_recv.at[q],
-                device_id={"col": peer},
+                device_id={"col": there * 4 + corner},
                 device_id_type=MESH,
             ).start()
             return 0
 
-        pltpu.make_async_copy(rowout.at[q, c], home2.at[q, tile(c * 16, 16)], z_recv.at[q]).start()
-        lax.fori_loop(1, nc, one, 0)
+        pltpu.make_async_copy(rowout.at[q, z], home2.at[q, z], z_recv.at[q]).start()
+        lax.fori_loop(1, nz, one, 0)
 
     def turn(q):
         pltpu.make_async_copy(home2.at[q], home2.at[q], z_recv.at[q]).wait()
         for b in range(2):
-            moved = mm(perm_in[...], home2[q, b * 256 : (b + 1) * 256, :])
-            home2t[q, :, b * 32 : (b + 1) * 32, :] = moved.reshape(8, 32, width).astype(BF)
+            tiles = [home2[q, n, 2 * b + p] for p in range(2) for n in range(nz)]
+            moved = mm(perm_in[...], jnp.concatenate(tiles, axis=0))
+            moved = moved.reshape(8, 2, 16, width).astype(BF)
+            for n in range(8):
+                home2t[q, 4 * n + 2 * b : 4 * n + 2 * b + 2] = moved[n]
 
         def one(k, _):
-            peer = lax.rem(r + k, nr)
+            other = lax.rem(place + k, 4 * nr)
             pltpu.make_async_remote_copy(
-                src_ref=home2t.at[q, peer],
-                dst_ref=seqs.at[4 + q, tile(r * 64, 64)],
+                src_ref=home2t.at[q, other],
+                dst_ref=seqs.at[4 + q, tile(place * 16, 16)],
                 send_sem=c_send.at[q],
                 recv_sem=c_recv.at[q],
-                device_id={"row": peer},
+                device_id=in_plane(other),
                 device_id_type=MESH,
             ).start()
             return 0
 
         pltpu.make_async_copy(
-            home2t.at[q, r], seqs.at[4 + q, tile(r * 64, 64)], c_recv.at[q]
+            home2t.at[q, place], seqs.at[4 + q, tile(place * 16, 16)], c_recv.at[q]
         ).start()
-        lax.fori_loop(1, nr, one, 0)
+        lax.fori_loop(1, 4 * nr, one, 0)
 
     def send_home(q):
         def one(k, _):
@@ -165,13 +177,13 @@
         ).start()
         lax.fori_loop(1, nr, one, 0)
 
-    lane_head = lax.shift_right_logical(
+    lane_head = shr(
         lax.broadcasted_iota(jnp.int32, (1, width), 1), int(math.log2(size))
     )
     zero, one_ = jnp.zeros((), BF), jnp.ones((), BF)
 
     def attention(t):
-        which = lax.shift_right_logical(t, 2)
+        which = shr(t, 2)
         for b in range(0, length, 256):
             normed = rms(seqs[t, b : b + 256, :].astype(F32)).astype(BF)
             mixed = mm(normed, wqkv[which])
@@ -220,7 +232,9 @@
                 for n in range(8)
             ]
             moved = mm(perm_out[...], jnp.concatenate(parts, axis=0))
-            out_ref[m, b * 16 : (b + 1) * 16] = moved.reshape(16, 16, width).astype(BF)
+            moved = moved.reshape(16, 16, width).astype(BF)
+            for n in range(8):
+                out_ref[m, n * 8 + 2 * b : n * 8 + 2 * b + 2] = moved[2 * n : 2 * n + 2]
 
     weight_copies_done = [False]
     for copy in weight_copies:
@@ -248,31 +262,37 @@
             second = done.reshape(32, 2, 8, width)
             for j in range(2):
                 both = jnp.concatenate([first[:, j], second[:, j]], axis=1)
-                rowout[q + j] = both.astype(BF)
+                rowout[q + j] = both.astype(BF).reshape(rowout.shape[1:])
             send_back(q)
             send_back(q + 1)
 
+        @pl.when(t >= 4)
+        def _():
+            colout[t - 4] = done.astype(BF)
+            send_home(t - 4)
+
         @pl.when(t == 3)
         def _():
             turn(0)
             turn(1)
 
-        @pl.when(t >= 4)
-        def _():
-            colout[t - 4] = done.astype(BF)
-            send_home(t - 4)
+        @pl.when(t == 4)
+        def _():
+            turn(2)
 
         @pl.when(t == 5)
         def _():
+            turn(3)
+
+        @pl.when(t == 6)
+        def _():
             feed_forward(0)
-            feed_forward(1)
-            finish(0)
-            turn(2)
-            turn(3)
 
         return 0
 
     lax.fori_loop(0, 8, step, 0)
+    feed_forward(1)
+    finish(0)
     feed_forward(2)
     feed_forward(3)
     finish(1)
@@ -280,8 +300,8 @@
     def drain(q, _):
         for ref, sem, rows in (
             (seqs, in_send, (nc - 1) * 16),
-            (home2, z_send, (nc - 1) * 16),
-            (colout, c_send, (nr - 1) * 64),
+            (home2, z_send, nz - 1),
+            (seqs, c_send, (4 * nr - 1) * 16),
             (home3, b_send, (nr - 1) * 64),
         ):
             view = ref.at[q, pl.ds(0, rows)]
@@ -299,7 +319,7 @@
         ff = weights[4].shape[1]
         dma4 = pltpu.SemaphoreType.DMA((4,))
         return pl.pallas_call(
-            functools.partial(kernel, nr, nc),
+            functools.partial(kernel, nr, nc, nc // 4),
             out_shape=jax.ShapeDtypeStruct(cells.shape, BF),
             in_specs=[pl.BlockSpec(memory_space=pl.ANY)] * 7,
             out_specs=pl.BlockSpec(memory_space=pltpu.VMEM),
@@ -310,9 +330,9 @@
                 pltpu.VMEM((ff, width), BF),
                 pltpu.VMEM((8, 512, width), BF),
                 pltpu.VMEM((512, width), F32),
-                pltpu.VMEM((4, 32, 16, width), BF),
-                pltpu.VMEM((4, 512, width), BF),
-                pltpu.VMEM((4, 8, 64, width), BF),
+                pltpu.VMEM((4, nc // 4, 4, 16, width), BF),
+                pltpu.VMEM((4, nc // 4, 4, 16, width), BF),
+                pltpu.VMEM((4, 4 * nr, 16, width), BF),
                 pltpu.VMEM((4, 512, width), BF),
                 pltpu.VMEM((4, 512, width), BF),
                 pltpu.VMEM((4, 512, width), BF),

time: 90.4 us -> 80.8 us (0.89)
  Pallas kernels: 87.4 us -> 78.4 us
    pallas_call x1, Pallas kernels: 87.4 us -> 78.4 us  [body(): pl.pallas_call(functools.partial(kernel, nr, nc, nc // 4), out_shape=jax....]
where the time goes in v2:
time: 80.8 us; the launch traced here: 80.7 us
  Pallas kernels  78.4 us (97%)
  local copies, waits for them, and re-layouts  2.26 us (3%)
    pallas_call x1, Pallas kernels, body(): pl.pallas_call(functools.partial(kernel, nr, nc, nc // 4), out_shape=jax....  78.4 us
    unnamed x1, local copies, waits for them, and re-layouts  2.26 us

profile of v2, /device:TPU:1, one launch (start us, length us, event | category | flops | bytes accessed | tf_op | source)
XLA Modules:
  0.0 80.7 jit_solution(11743357232633868622)
XLA Ops:
  0.0 78.4 %axial.1 = bf16[2,64,16,256]{3,2,1,0:T(8,128)(2,1)} custom-call(bf16[2,64,16,256]{3,2,1,0:T(8,128)(2,1)} %x_hbm.1, bf16[256,768]{1,0:T(8,128)(2,1)} %wrq.1, bf16[256,256]{1,0:T(8,128)(2,1)} %wro.1, bf16[256,768]{1,0:T(8,128)(2,1)} %wcq.1, bf16[256,256]{1,0:T(8,128)(2,1)} %wco.1, bf16[256,1024]{1,0:T(8,128)(2,1)} %wup.1, bf16[1024,256]{1,0:T(8,128)(2,1)} %wdn.1), custom_call_target="tpu_custom_call" | custom-call | tf_op jit(solution)/shard_map/axial/pallas_call | solution.py:321
  78.4 2.3 %copy.9 = bf16[2,64,16,256]{3,2,1,0:T(8,128)(2,1)} copy(bf16[2,64,16,256]{3,2,1,0:T(8,128)(2,1)} %axial.1) | data formatting | bytes 2097152

commit v3 on v2

--- a/solution.py
+++ b/solution.py
@@ -42,9 +42,9 @@
     nr, nc, nz,
     x_hbm, wrq, wro, wcq, wco, wup, wdn,
     out_ref,
-    wqkv, wo, up, down, seqs, stash, rowout, home2, home2t, colout, home3, res,
-    q_s, k_s, w_s, perm_in, perm_out,
-    w_sem, in_send, in_recv, z_send, z_recv, c_send, c_recv, b_send, b_recv,
+    wqkv, wo, up, down, seqs, rowres, rowout, relay, relayed, colout, home3, res,
+    q_s, k_s, w_s, perm_a, perm_b,
+    w_sem, in_send, in_recv, p_send, p_recv, c_send, c_recv, b_send, b_recv,
 ):
     r = lax.axis_index("row")
     c = lax.axis_index("col")
@@ -87,8 +87,8 @@
 
     lax.fori_loop(1, nc, greet_col, 0)
     lax.fori_loop(1, 4 * nr, greet_plane, 0)
-    permutation(perm_in, lambda o: (shr(o, 4) & 1) * 128 + (o & 15) * 8 + shr(o, 5))
-    permutation(perm_out, lambda o: (o & 15) * 16 + shr(o, 4))
+    permutation(perm_a, lambda o: (o & 15) * 16 + shr(o, 4))
+    permutation(perm_b, lambda o: (o & 31) * 8 + shr(o, 5))
     pl.semaphore_wait(barrier, nc - 1 + 4 * nr - 1)
 
     def tile(base, n):
@@ -98,7 +98,7 @@
         m, i = shr(s, 1), s & 1
 
         def one(k, _):
-            peer = lax.rem(c + k, nc)
+            peer = lax.rem(c + nc + (1 - 2 * (k & 1)) * shr(k + 1, 1), nc)
             pltpu.make_async_remote_copy(
                 src_ref=x_hbm.at[m, 2 * peer + i],
                 dst_ref=seqs.at[s, tile(c * 16, 16)],
@@ -117,51 +117,64 @@
 
     lax.fori_loop(0, 4, send_in, 0)
 
-    def send_back(q):
+    def split(m):
+        for b in range(4):
+            tiles = [
+                rowres[i, n * 64 + b * 16 : n * 64 + b * 16 + 16, :]
+                for i in range(2)
+                for n in range(nz)
+            ]
+            moved = mm(perm_a[...], jnp.concatenate(tiles, axis=0))
+            moved = moved.reshape(2, 8, 16, width).astype(BF)
+            for j in range(2):
+                for n in range(8):
+                    rowout[2 * m + j, 4 * n + b] = moved[j, n]
+
+    def across(q):
+        def one(k, _):
+            other = place ^ (4 * nr - k)
+            pltpu.make_async_remote_copy(
+                src_ref=rowout.at[q, other],
+                dst_ref=relay.at[q, tile(place * 16, 16)],
+                send_sem=p_send.at[q],
+                recv_sem=p_recv.at[q],
+                device_id=in_plane(other),
+                device_id_type=MESH,
+            ).start()
+            return 0
+
+        pltpu.make_async_copy(
+            rowout.at[q, place], relay.at[q, tile(place * 16, 16)], p_recv.at[q]
+        ).start()
+        lax.fori_loop(1, 4 * nr, one, 0)
+
+    def forward(q):
+        pltpu.make_async_copy(relay.at[q], relay.at[q], p_recv.at[q]).wait()
+        for b in range(2):
+            moved = mm(perm_b[...], relay[q, b * 256 : (b + 1) * 256, :])
+            moved = moved.reshape(nz, 32, width).astype(BF)
+            relayed[q, :, b * 32 : (b + 1) * 32, :] = moved
+
         def one(k, _):
             there = lax.rem(z + k, nz)
             pltpu.make_async_remote_copy(
-                src_ref=rowout.at[q, there],
-                dst_ref=home2.at[q, z],
-                send_sem=z_send.at[q],
-                recv_sem=z_recv.at[q],
+                src_ref=relayed.at[q, there],
+                dst_ref=seqs.at[4 + q, tile(z * 64, 64)],
+                send_sem=c_send.at[q],
+                recv_sem=c_recv.at[q],
                 device_id={"col": there * 4 + corner},
                 device_id_type=MESH,
             ).start()
             return 0
 
-        pltpu.make_async_copy(rowout.at[q, z], home2.at[q, z], z_recv.at[q]).start()
+        pltpu.make_async_copy(
+            relayed.at[q, z], seqs.at[4 + q, tile(z * 64, 64)], c_recv.at[q]
+        ).start()
         lax.fori_loop(1, nz, one, 0)
-
-    def turn(q):
-        pltpu.make_async_copy(home2.at[q], home2.at[q], z_recv.at[q]).wait()
-        for b in range(2):
-            tiles = [home2[q, n, 2 * b + p] for p in range(2) for n in range(nz)]
-            moved = mm(perm_in[...], jnp.concatenate(tiles, axis=0))
-            moved = moved.reshape(8, 2, 16, width).astype(BF)
-            for n in range(8):
-                home2t[q, 4 * n + 2 * b : 4 * n + 2 * b + 2] = moved[n]
-
-        def one(k, _):
-            other = lax.rem(place + k, 4 * nr)
-            pltpu.make_async_remote_copy(
-                src_ref=home2t.at[q, other],
-                dst_ref=seqs.at[4 + q, tile(place * 16, 16)],
-                send_sem=c_send.at[q],
-                recv_sem=c_recv.at[q],
-                device_id=in_plane(other),
-                device_id_type=MESH,
-            ).start()
-            return 0
-
-        pltpu.make_async_copy(
-            home2t.at[q, place], seqs.at[4 + q, tile(place * 16, 16)], c_recv.at[q]
-        ).start()
-        lax.fori_loop(1, 4 * nr, one, 0)
 
     def send_home(q):
         def one(k, _):
-            peer = lax.rem(r + k, nr)
+            peer = r ^ (nr - k)
             pltpu.make_async_remote_copy(
                 src_ref=colout.at[q, tile(peer * 64, 64)],
                 dst_ref=home3.at[q, tile(r * 64, 64)],
@@ -231,12 +244,9 @@
                 for j in range(2)
                 for n in range(8)
             ]
-            moved = mm(perm_out[...], jnp.concatenate(parts, axis=0))
-            moved = moved.reshape(16, 16, width).astype(BF)
-            for n in range(8):
-                out_ref[m, n * 8 + 2 * b : n * 8 + 2 * b + 2] = moved[2 * n : 2 * n + 2]
-
-    weight_copies_done = [False]
+            moved = mm(perm_a[...], jnp.concatenate(parts, axis=0))
+            out_ref[m, b * 16 : (b + 1) * 16] = moved.reshape(16, 16, width).astype(BF)
+
     for copy in weight_copies:
         copy.wait()
 
@@ -251,48 +261,52 @@
 
         done = attention(t)
 
-        @pl.when((t < 4) & ((t & 1) == 0))
-        def _():
-            stash[...] = done
-
-        @pl.when((t < 4) & ((t & 1) == 1))
-        def _():
-            q = t - 1
-            first = stash[...].reshape(32, 2, 8, width)
-            second = done.reshape(32, 2, 8, width)
-            for j in range(2):
-                both = jnp.concatenate([first[:, j], second[:, j]], axis=1)
-                rowout[q + j] = both.astype(BF).reshape(rowout.shape[1:])
-            send_back(q)
-            send_back(q + 1)
+        @pl.when(t < 4)
+        def _():
+            rowres[t & 1] = done.astype(BF)
 
         @pl.when(t >= 4)
         def _():
-            colout[t - 4] = done.astype(BF)
+            pieces = [
+                done[n * 64 + p * 8 : n * 64 + p * 8 + 8, :] for p in range(nr) for n in range(nz)
+            ]
+            colout[t - 4] = jnp.concatenate(pieces, axis=0).astype(BF)
             send_home(t - 4)
 
+        @pl.when(t == 1)
+        def _():
+            split(0)
+            across(0)
+
+        @pl.when(t == 2)
+        def _():
+            across(1)
+            forward(0)
+
         @pl.when(t == 3)
         def _():
-            turn(0)
-            turn(1)
+            split(1)
+            across(2)
+            forward(1)
+            across(3)
 
         @pl.when(t == 4)
         def _():
-            turn(2)
+            forward(2)
 
         @pl.when(t == 5)
         def _():
-            turn(3)
+            forward(3)
+            feed_forward(0)
 
         @pl.when(t == 6)
         def _():
-            feed_forward(0)
+            feed_forward(1)
+            finish(0)
 
         return 0
 
     lax.fori_loop(0, 8, step, 0)
-    feed_forward(1)
-    finish(0)
     feed_forward(2)
     feed_forward(3)
     finish(1)
@@ -300,8 +314,8 @@
     def drain(q, _):
         for ref, sem, rows in (
             (seqs, in_send, (nc - 1) * 16),
-            (home2, z_send, nz - 1),
-            (seqs, c_send, (4 * nr - 1) * 16),
+            (seqs, p_send, (4 * nr - 1) * 16),
+            (seqs, c_send, (nz - 1) * 64),
             (home3, b_send, (nr - 1) * 64),
         ):
             view = ref.at[q, pl.ds(0, rows)]
@@ -329,10 +343,10 @@
                 pltpu.VMEM((width, ff), BF),
                 pltpu.VMEM((ff, width), BF),
                 pltpu.VMEM((8, 512, width), BF),
-                pltpu.VMEM((512, width), F32),
-                pltpu.VMEM((4, nc // 4, 4, 16, width), BF),
-                pltpu.VMEM((4, nc // 4, 4, 16, width), BF),
+                pltpu.VMEM((2, 512, width), BF),
                 pltpu.VMEM((4, 4 * nr, 16, width), BF),
+                pltpu.VMEM((4, 512, width), BF),
+                pltpu.VMEM((4, nc // 4, 64, width), BF),
                 pltpu.VMEM((4, 512, width), BF),
                 pltpu.VMEM((4, 512, width), BF),
                 pltpu.VMEM((4, 512, width), BF),

time: 80.8 us -> 76.1 us (0.942)
  Pallas kernels: 78.4 us -> 73.7 us
    pallas_call x1, Pallas kernels: 78.4 us -> 73.7 us  [body(): pl.pallas_call(functools.partial(kernel, nr, nc, nc // 4), out_shape=jax....]
where the time goes in v3:
time: 76.1 us; the launch traced here: 76 us
  Pallas kernels  73.7 us (97%)
  local copies, waits for them, and re-layouts  2.26 us (3%)
    pallas_call x1, Pallas kernels, body(): pl.pallas_call(functools.partial(kernel, nr, nc, nc // 4), out_shape=jax....  73.7 us
    unnamed x1, local copies, waits for them, and re-layouts  2.26 us

profile of v3, /device:TPU:1, one launch (start us, length us, event | category | flops | bytes accessed | tf_op | source)
XLA Modules:
  0.0 76.0 jit_solution(9126435280084749426)
XLA Ops:
  0.0 73.7 %axial.1 = bf16[2,64,16,256]{3,2,1,0:T(8,128)(2,1)} custom-call(bf16[2,64,16,256]{3,2,1,0:T(8,128)(2,1)} %x_hbm.1, bf16[256,768]{1,0:T(8,128)(2,1)} %wrq.1, bf16[256,256]{1,0:T(8,128)(2,1)} %wro.1, bf16[256,768]{1,0:T(8,128)(2,1)} %wcq.1, bf16[256,256]{1,0:T(8,128)(2,1)} %wco.1, bf16[256,1024]{1,0:T(8,128)(2,1)} %wup.1, bf16[1024,256]{1,0:T(8,128)(2,1)} %wdn.1), custom_call_target="tpu_custom_call" | custom-call | tf_op jit(solution)/shard_map/axial/pallas_call | solution.py:335
  73.7 2.3 %copy.9 = bf16[2,64,16,256]{3,2,1,0:T(8,128)(2,1)} copy(bf16[2,64,16,256]{3,2,1,0:T(8,128)(2,1)} %axial.1) | data formatting | bytes 2097152

commit v4 on v3

--- a/solution.py
+++ b/solution.py
@@ -43,8 +43,8 @@
     x_hbm, wrq, wro, wcq, wco, wup, wdn,
     out_ref,
     wqkv, wo, up, down, seqs, rowres, rowout, relay, relayed, colout, home3, res,
-    q_s, k_s, w_s, perm_a, perm_b,
-    w_sem, in_send, in_recv, p_send, p_recv, c_send, c_recv, b_send, b_recv,
+    q_s, k_s, w_s, perm_a, perm_b, out_v,
+    w_sem, o_sem, in_send, in_recv, p_send, p_recv, c_send, c_recv, b_send, b_recv,
 ):
     r = lax.axis_index("row")
     c = lax.axis_index("col")
@@ -237,6 +237,10 @@
             hidden = jax.nn.gelu(mm(rms(y).astype(BF), up[...]), approximate=True)
             res[q, b : b + 256, :] = (y + mm(hidden.astype(BF), down[...])).astype(BF)
 
+    def out_copy(m, b):
+        rows = pl.ds(b * 16, 16)
+        return pltpu.make_async_copy(out_v.at[m, rows], out_ref.at[m, rows], o_sem.at[m, b])
+
     def finish(m):
         for b in range(4):
             parts = [
@@ -245,7 +249,8 @@
                 for n in range(8)
             ]
             moved = mm(perm_a[...], jnp.concatenate(parts, axis=0))
-            out_ref[m, b * 16 : (b + 1) * 16] = moved.reshape(16, 16, width).astype(BF)
+            out_v[m, b * 16 : (b + 1) * 16] = moved.reshape(16, 16, width).astype(BF)
+            out_copy(m, b).start()
 
     for copy in weight_copies:
         copy.wait()
@@ -287,26 +292,23 @@
         def _():
             split(1)
             across(2)
+            across(3)
             forward(1)
-            across(3)
+            forward(2)
 
         @pl.when(t == 4)
         def _():
-            forward(2)
+            forward(3)
 
         @pl.when(t == 5)
         def _():
-            forward(3)
             feed_forward(0)
 
-        @pl.when(t == 6)
-        def _():
-            feed_forward(1)
-            finish(0)
-
         return 0
 
     lax.fori_loop(0, 8, step, 0)
+    feed_forward(1)
+    finish(0)
     feed_forward(2)
     feed_forward(3)
     finish(1)
@@ -323,6 +325,9 @@
         return 0
 
     lax.fori_loop(0, 4, drain, 0)
+    for m in range(2):
+        for b in range(4):
+            out_copy(m, b).wait()
 
 
 def solution(mesh):
@@ -336,7 +341,7 @@
             functools.partial(kernel, nr, nc, nc // 4),
             out_shape=jax.ShapeDtypeStruct(cells.shape, BF),
             in_specs=[pl.BlockSpec(memory_space=pl.ANY)] * 7,
-            out_specs=pl.BlockSpec(memory_space=pltpu.VMEM),
+            out_specs=pl.BlockSpec(memory_space=pl.ANY),
             scratch_shapes=[
                 pltpu.VMEM((2, width, 3 * width), BF),
                 pltpu.VMEM((2, width, width), BF),
@@ -355,7 +360,9 @@
                 pltpu.VMEM((HEADS * 512, width), BF),
                 pltpu.VMEM((256, 256), BF),
                 pltpu.VMEM((256, 256), BF),
+                pltpu.VMEM(cells.shape, BF),
                 pltpu.SemaphoreType.DMA((6,)),
+                pltpu.SemaphoreType.DMA((2, 4)),
             ]
             + [dma4] * 8,
             compiler_params=pltpu.CompilerParams(

time: 76.1 us -> 75.3 us (0.989)
  Pallas kernels: 73.7 us -> 72.4 us
    pallas_call x1, Pallas kernels: 73.7 us -> 72.4 us  [body(): pl.pallas_call(functools.partial(kernel, nr, nc, nc // 4), out_shape=jax....]
where the time goes in v4:
time: 75.3 us; the launch traced here: 74.6 us
  Pallas kernels  72.4 us (96%)
  local copies, waits for them, and re-layouts  2.26 us (3%)
    pallas_call x1, Pallas kernels, body(): pl.pallas_call(functools.partial(kernel, nr, nc, nc // 4), out_shape=jax....  72.4 us
    unnamed x1, local copies, waits for them, and re-layouts  2.26 us

profile of v4, /device:TPU:1, one launch (start us, length us, event | category | flops | bytes accessed | tf_op | source)
XLA Modules:
  0.0 74.6 jit_solution(6364012910663242327)
XLA Ops:
  0.0 72.4 %axial.1 = bf16[2,64,16,256]{3,2,1,0:T(8,128)(2,1)} custom-call(bf16[2,64,16,256]{3,2,1,0:T(8,128)(2,1)} %x_hbm.1, bf16[256,768]{1,0:T(8,128)(2,1)} %wrq.1, bf16[256,256]{1,0:T(8,128)(2,1)} %wro.1, bf16[256,768]{1,0:T(8,128)(2,1)} %wcq.1, bf16[256,256]{1,0:T(8,128)(2,1)} %wco.1, bf16[256,1024]{1,0:T(8,128)(2,1)} %wup.1, bf16[1024,256]{1,0:T(8,128)(2,1)} %wdn.1), custom_call_target="tpu_custom_call" | custom-call | tf_op jit(solution)/shard_map/axial/pallas_call | solution.py:340
  72.4 2.3 %copy.9 = bf16[2,64,16,256]{3,2,1,0:T(8,128)(2,1)} copy(bf16[2,64,16,256]{3,2,1,0:T(8,128)(2,1)} %axial.1) | data formatting | bytes 2097152

commit v5 on v4

--- a/solution.py
+++ b/solution.py
@@ -112,7 +112,7 @@
         pltpu.make_async_copy(
             x_hbm.at[m, 2 * c + i], seqs.at[s, tile(c * 16, 16)], in_recv.at[s]
         ).start()
-        lax.fori_loop(1, nc, one, 0)
+        lax.fori_loop(1, nc, one, 0, unroll=True)
         return 0
 
     lax.fori_loop(0, 4, send_in, 0)
@@ -146,7 +146,7 @@
         pltpu.make_async_copy(
             rowout.at[q, place], relay.at[q, tile(place * 16, 16)], p_recv.at[q]
         ).start()
-        lax.fori_loop(1, 4 * nr, one, 0)
+        lax.fori_loop(1, 4 * nr, one, 0, unroll=True)
 
     def forward(q):
         pltpu.make_async_copy(relay.at[q], relay.at[q], p_recv.at[q]).wait()

time: 75.3 us -> 75.5 us (level)
  no operation moved by 1% of the time
where the time goes in v5:
time: 75.5 us; the launch traced here: 75.4 us
  Pallas kernels  73.1 us (97%)
  local copies, waits for them, and re-layouts  2.26 us (3%)
    pallas_call x1, Pallas kernels, body(): pl.pallas_call(functools.partial(kernel, nr, nc, nc // 4), out_shape=jax....  73.1 us
    unnamed x1, local copies, waits for them, and re-layouts  2.26 us

profile of v5, /device:TPU:1, one launch (start us, length us, event | category | flops | bytes accessed | tf_op | source)
XLA Modules:
  0.0 75.4 jit_solution(3594322915314121332)
XLA Ops:
  0.0 73.1 %axial.1 = bf16[2,64,16,256]{3,2,1,0:T(8,128)(2,1)} custom-call(bf16[2,64,16,256]{3,2,1,0:T(8,128)(2,1)} %x_hbm.1, bf16[256,768]{1,0:T(8,128)(2,1)} %wrq.1, bf16[256,256]{1,0:T(8,128)(2,1)} %wro.1, bf16[256,768]{1,0:T(8,128)(2,1)} %wcq.1, bf16[256,256]{1,0:T(8,128)(2,1)} %wco.1, bf16[256,1024]{1,0:T(8,128)(2,1)} %wup.1, bf16[1024,256]{1,0:T(8,128)(2,1)} %wdn.1), custom_call_target="tpu_custom_call" | custom-call | tf_op jit(solution)/shard_map/axial/pallas_call | solution.py:340
  73.1 2.3 %copy.9 = bf16[2,64,16,256]{3,2,1,0:T(8,128)(2,1)} copy(bf16[2,64,16,256]{3,2,1,0:T(8,128)(2,1)} %axial.1) | data formatting | bytes 2097152
